TPU v7x, 512 devices: a whole 4x4x16 slice. The times are simulated.
512 devices in a mesh: gx: 16 (over z), gy: 8 (over x, core), gz: 4 (over y).
Axes of the slice: x: 4, y: 4, z: 16, core: 2. Of those that a mesh axis runs over, the one named last changes fastest.
Arguments:
- field: float32 [2, 256, 512, 512], P(None, 'gx', 'gy', 'gz'), may hold values from -24 to 24
Outputs:
- core: float32 [2, 256, 512, 128], P(None, 'gx', ('gy', 'gz'))
- factor: float32 [512, 128], replicated
All inputs are finite; a program needn't handle non-finite values.
Results may differ from a plain program's by a relative error of at most 0.0003.
Values sent between devices are 32-bit elements; how exact they have to be, the bound alone decides.
A program may use at most 64 MiB of HBM per device.

v0:
```python
import functools

import jax
import jax.numpy as jnp
from jax import lax
from jax.experimental import pallas as pl
from jax.experimental.pallas import tpu as pltpu
from jax.sharding import PartitionSpec as P

RANK = 128
ITERS = 4
LANES = 128
PANEL = 32
VMEM = pl.BlockSpec(memory_space=pltpu.VMEM)


def full_dot(a, b, ca, cb):
    return lax.dot_general(
        a,
        b,
        (((ca,), (cb,)), ((), ())),
        precision=lax.Precision.HIGHEST,
        preferred_element_type=jnp.float32,
    )


def block_pairs(blocks):
    return [(i, j) for i in range(blocks) for j in range(i, blocks)]


def gather_kernel(
    sizes, total_rows, field, fib, gram, acc, half, core_in, plane_in, mine, z_in, z_sum, plane_all, all_rows,
    own_sem, a2a_send, a2a_recv, core_send, core_recv, plane_send, plane_recv, z_send, z_recv,
    zg_send, zg_recv, pg_send, pg_recv, cg_send, cg_recv,
):
    nz, nx, ny = sizes
    planes = nx * ny
    blocks = ny
    pairs = block_pairs(blocks)
    cells = fib.shape[3]
    steps = fib.shape[1]
    half_rows = half.shape[0]
    piece = plane_in.shape[1]
    tiles = piece // 8
    z = lax.axis_index("gx")
    gy = lax.axis_index("gy")
    x = gy // 2
    c = gy % 2
    y = lax.axis_index("gz")
    p = x * ny + y

    def peer_plane(k):
        q = lax.rem(p + k, planes)
        return q, {"gy": (q // ny) * 2 + c, "gz": lax.rem(q, ny)}

    other = {"gy": x * 2 + (1 - c)}

    barrier = pltpu.get_barrier_semaphore()
    pl.semaphore_signal(barrier, inc=1, device_id=other)

    def greet_plane(k, _):
        pl.semaphore_signal(barrier, inc=1, device_id=peer_plane(k)[1])
        return 0

    def greet_z(k, _):
        pl.semaphore_signal(barrier, inc=1, device_id={"gx": lax.rem(z + k, nz)})
        return 0

    lax.fori_loop(1, planes, greet_plane, 0)
    lax.fori_loop(1, nz, greet_z, 0)
    pl.semaphore_wait(barrier, planes + nz - 1)

    sends = []
    for s in range(steps):
        for k in range(1, ny):
            to = lax.rem(y + k, ny)
            copy = pltpu.make_async_remote_copy(
                src_ref=field.at[s, :, pl.ds(to * cells, cells), :],
                dst_ref=fib.at[y, s],
                send_sem=a2a_send.at[s, k - 1],
                recv_sem=a2a_recv.at[s, k - 1],
                device_id={"gz": to},
            )
            copy.start()
            sends.append(copy)
    owns = []
    for s in range(steps):
        copy = pltpu.make_async_copy(field.at[s, :, pl.ds(y * cells, cells), :], fib.at[y, s], own_sem.at[s])
        copy.start()
        owns.append(copy)
    for s in range(steps):
        owns[s].wait()
        for k in range(1, ny):
            sends[s * (ny - 1) + k - 1].wait_recv()
        rows = jnp.concatenate([fib[b, s].reshape(-1, LANES) for b in range(blocks)], axis=1)
        for i in range(0, blocks, 2):
            term = full_dot(rows[:, i * LANES : (i + 2) * LANES], rows[:, i * LANES :], 0, 0)
            for a in (0, 1):
                for b in range(i + a, blocks):
                    n = pairs.index((i + a, b)) * LANES
                    part = term[a * LANES : (a + 1) * LANES, (b - i) * LANES : (b - i + 1) * LANES]
                    if s == 0:
                        acc[n : n + LANES, :] = part
                    else:
                        acc[n : n + LANES, :] = acc[n : n + LANES, :] + part

    keep = pl.multiple_of(c * half_rows, 8)
    give = pl.multiple_of((1 - c) * half_rows, 8)
    copy = pltpu.make_async_remote_copy(
        src_ref=acc.at[pl.ds(give, half_rows)],
        dst_ref=core_in,
        send_sem=core_send,
        recv_sem=core_recv,
        device_id=other,
    )
    copy.start()
    copy.wait_recv()
    half[...] = acc[pl.ds(keep, half_rows), :] + core_in[...]
    copy.wait_send()

    def plane_copy(k):
        q, device = peer_plane(k)
        return pltpu.make_async_remote_copy(
            src_ref=half.at[pl.ds(pl.multiple_of(q * piece, 8), piece)],
            dst_ref=plane_in.at[k - 1],
            send_sem=plane_send.at[k - 1],
            recv_sem=plane_recv.at[k - 1],
            device_id=device,
        )

    def start(make):
        def body(k, _):
            make(k).start()
            return 0

        return body

    def finish(make):
        def body(k, _):
            make(k).wait_send()
            return 0

        return body

    lax.fori_loop(1, planes, start(plane_copy), 0)

    def plane_add(k, total):
        plane_copy(k).wait_recv()
        return total + plane_in[k - 1]

    mine[...] = lax.fori_loop(1, planes, plane_add, half[pl.ds(pl.multiple_of(p * piece, 8), piece), :])

    spread = nz // tiles
    tile = lax.rem(z // spread, tiles)
    owner = (lax.rem(z, spread) == 0) & (z // spread < tiles)

    def z_copy(t):
        return pltpu.make_async_remote_copy(
            src_ref=mine.at[pl.ds(t * 8, 8)],
            dst_ref=z_in.at[z],
            send_sem=z_send.at[t],
            recv_sem=z_recv.at[z],
            device_id={"gx": t * spread},
        )

    for t in range(tiles):

        @pl.when(z != t * spread)
        def _():
            z_copy(t).start()

    @pl.when(owner)
    def _():
        def z_add(k, total):
            w = lax.rem(z + k, nz)
            pltpu.make_async_remote_copy(
                src_ref=z_in.at[w],
                dst_ref=z_in.at[w],
                send_sem=z_send.at[0],
                recv_sem=z_recv.at[w],
                device_id={"gx": w},
            ).wait_recv()
            return total + z_in[w]

        own = mine[pl.ds(pl.multiple_of(tile * 8, 8), 8), :]
        z_sum[tile] = lax.fori_loop(1, nz, z_add, own) * jnp.float32(1.0 / total_rows)

    def zg_copy(k):
        return pltpu.make_async_remote_copy(
            src_ref=z_sum.at[tile],
            dst_ref=z_sum.at[tile],
            send_sem=zg_send.at[k - 1],
            recv_sem=zg_recv.at[tile],
            device_id={"gx": lax.rem(z + k, nz)},
        )

    @pl.when(owner)
    def _():
        lax.fori_loop(1, nz, start(zg_copy), 0)

    for t in range(tiles):

        @pl.when(z != t * spread)
        def _():
            pltpu.make_async_remote_copy(
                src_ref=z_sum.at[t],
                dst_ref=z_sum.at[t],
                send_sem=zg_send.at[0],
                recv_sem=zg_recv.at[t],
                device_id={"gx": lax.rem(z + 1, nz)},
            ).wait_recv()

    plane_all[p] = z_sum[...].reshape(piece, LANES)

    def pg_copy(k):
        return pltpu.make_async_remote_copy(
            src_ref=plane_all.at[p],
            dst_ref=plane_all.at[p],
            send_sem=pg_send.at[k - 1],
            recv_sem=pg_recv.at[k - 1],
            device_id=peer_plane(k)[1],
        )

    def cg_copy(k):
        q = lax.rem(p + planes - k, planes)
        return pltpu.make_async_remote_copy(
            src_ref=plane_all.at[q],
            dst_ref=all_rows.at[q],
            send_sem=cg_send.at[k],
            recv_sem=cg_recv.at[k],
            device_id=other,
        )

    lax.fori_loop(1, planes, start(pg_copy), 0)
    cg_copy(0).start()

    def forward(k, _):
        pg_copy(k).wait_recv()
        cg_copy(k).start()
        return 0

    lax.fori_loop(1, planes, forward, 0)

    def arrived(k, _):
        cg_copy(k).wait_recv()
        return 0

    lax.fori_loop(0, planes, arrived, 0)

    def put(n, block):
        i, j = pairs[n]
        gram[i * LANES : (i + 1) * LANES, j * LANES : (j + 1) * LANES] = block
        if i != j:
            gram[j * LANES : (j + 1) * LANES, i * LANES : (i + 1) * LANES] = block.T

    here = plane_all[...].reshape(half_rows, LANES)
    there = all_rows[...].reshape(half_rows, LANES)
    low = jnp.where(c == 0, here, there)
    high = jnp.where(c == 0, there, here)
    both = jnp.concatenate([low, high], axis=0)
    for n in range(len(pairs)):
        put(n, both[n * LANES : (n + 1) * LANES, :])

    for copy in sends:
        copy.wait_send()
    lax.fori_loop(1, planes, finish(plane_copy), 0)
    for t in range(tiles):

        @pl.when(z != t * spread)
        def _():
            z_copy(t).wait_send()

    @pl.when(owner)
    def _():
        lax.fori_loop(1, nz, finish(zg_copy), 0)

    lax.fori_loop(1, planes, finish(pg_copy), 0)
    lax.fori_loop(0, planes, finish(cg_copy), 0)


def reciprocal(d):
    r = pl.reciprocal(d, approx=True)
    return r * (2.0 - d * r)


def eliminate(w, factor_t):
    wide = w.shape[1]
    rank = w.shape[0]
    groups = PANEL // 8
    rows = lax.broadcasted_iota(jnp.int32, (8, LANES), 0)

    def spread(v):
        return jnp.concatenate([v] * (wide // LANES), axis=1)

    def row(v, i):
        return jnp.broadcast_to(v[i : i + 1, :], (8, v.shape[1]))

    for j0 in range(0, rank, PANEL):
        panel = [w[j0 + 8 * g : j0 + 8 * g + 8, :] for g in range(groups)]
        cols = {}
        for k in range(PANEL):
            for g in range(k // 8, groups):
                cols[k, g] = jnp.broadcast_to(panel[g][:, j0 + k : j0 + k + 1], (8, LANES))
        scale = [jnp.ones((8, LANES), jnp.float32) for _ in range(groups)]
        for j in range(PANEL):
            gj, ij = j // 8, j % 8
            pivot = row(cols[j, gj], ij)
            inverse = reciprocal(pivot)
            if j + 1 < PANEL:
                k = j + 1
                across = row(cols[j, k // 8], k % 8)
                for g in range(k // 8, groups):
                    cols[k, g] = cols[k, g] - (cols[j, g] * across) * inverse
            multiplier = {g: cols[j, g] * inverse for g in range(gj, groups)}
            for k in range(j + 2, PANEL):
                across = row(cols[j, k // 8], k % 8)
                for g in range(k // 8, groups):
                    cols[k, g] = cols[k, g] - multiplier[g] * across
            pivot_row = row(panel[gj], ij)
            scale[gj] = jnp.where(rows == ij, lax.rsqrt(pivot), scale[gj])
            for g in range(gj, groups):
                if g > gj:
                    panel[g] = panel[g] - spread(multiplier[g]) * pivot_row
                elif ij < 7:
                    panel[g] = panel[g] - spread(jnp.where(rows > ij, multiplier[g], 0.0)) * pivot_row
        panel = [panel[g] * spread(scale[g]) for g in range(groups)]
        for g in range(groups):
            factor_t[j0 + 8 * g : j0 + 8 * g + 8, :] = panel[g][:, rank:]
        j1 = j0 + PANEL
        if j1 < rank:
            upper = jnp.concatenate(panel, axis=0)
            w[j1:, :] = w[j1:, :] - full_dot(upper[:, j1:rank], upper, 0, 0)


def factor_kernel(fib, gram, core, factor, w, factor_t):
    rank = w.shape[0]
    for step in range(ITERS):
        if step == 0:
            grown_t = gram[:rank, :]
        else:
            grown_t = full_dot(factor_t[...], gram[...], 1, 0)
        w[:, rank:] = grown_t
        w[:, :rank] = full_dot(grown_t, grown_t, 1, 1)
        eliminate(w, factor_t)
    result = factor_t[...].T
    factor[...] = result
    rows = jnp.concatenate([fib[b].reshape(-1, LANES) for b in range(fib.shape[0])], axis=1)
    core[...] = full_dot(rows, result, 1, 0)


def on_device(sizes, field):
    nz, nx, ny = sizes
    steps, width_x, width_y, width_z = field.shape
    cells = width_y // ny
    width = width_z * ny
    planes = nx * ny
    rows = steps * width_x * cells
    pair_rows = len(block_pairs(ny)) * LANES
    half = pair_rows // 2
    piece = half // planes
    tiles = piece // 8
    f32 = jnp.float32
    dma = pltpu.SemaphoreType.DMA
    fib, gram = pl.pallas_call(
        functools.partial(gather_kernel, sizes, rows * nz * nx * 2 * ny),
        out_shape=(
            jax.ShapeDtypeStruct((ny, steps, width_x, cells, width_z), f32),
            jax.ShapeDtypeStruct((width, width), f32),
        ),
        in_specs=[pl.BlockSpec(memory_space=pl.ANY)],
        out_specs=(VMEM, VMEM),
        scratch_shapes=[
            pltpu.VMEM((pair_rows, LANES), f32),
            pltpu.VMEM((half, LANES), f32),
            pltpu.VMEM((half, LANES), f32),
            pltpu.VMEM((planes - 1, piece, LANES), f32),
            pltpu.VMEM((piece, LANES), f32),
            pltpu.VMEM((nz, 8, LANES), f32),
            pltpu.VMEM((tiles, 8, LANES), f32),
            pltpu.VMEM((planes, piece, LANES), f32),
            pltpu.VMEM((planes, piece, LANES), f32),
            dma((steps,)),
            dma((steps, ny - 1)),
            dma((steps, ny - 1)),
            dma,
            dma,
            dma((planes - 1,)),
            dma((planes - 1,)),
            dma((tiles,)),
            dma((nz,)),
            dma((nz - 1,)),
            dma((tiles,)),
            dma((planes - 1,)),
            dma((planes - 1,)),
            dma((planes,)),
            dma((planes,)),
        ],
        compiler_params=pltpu.CompilerParams(
            collective_id=0, has_side_effects=True, vmem_limit_bytes=24 * 2**20
        ),
        name="gather_gram",
    )(field)
    core, factor = pl.pallas_call(
        factor_kernel,
        out_shape=(
            jax.ShapeDtypeStruct((rows, RANK), f32),
            jax.ShapeDtypeStruct((width, RANK), f32),
        ),
        in_specs=[VMEM, VMEM],
        out_specs=(VMEM, VMEM),
        scratch_shapes=[
            pltpu.VMEM((RANK, RANK + width), f32),
            pltpu.VMEM((RANK, width), f32),
        ],
        compiler_params=pltpu.CompilerParams(vmem_limit_bytes=24 * 2**20),
        name="factor_core",
    )(fib, gram)
    return core.reshape(steps, width_x, cells, RANK), factor


def solution(mesh):
    sizes = (mesh.shape["gx"], mesh.shape["gy"] // 2, mesh.shape["gz"])
    return jax.shard_map(
        functools.partial(on_device, sizes),
        mesh=mesh,
        in_specs=(P(None, "gx", "gy", "gz"),),
        out_specs=(P(None, "gx", ("gy", "gz"), None), P()),
        check_vma=False,
    )
```

profile of v0, /device:TPU:1, one launch (start us, length us, event | category | flops | bytes accessed | tf_op | source)
XLA Modules:
  0.0 87.9 jit_solution(28469353790215921)
XLA Ops:
  0.6 0.0 copy-start
  0.6 1.2 %copy-done = f32[2,16,64,128]{3,2,1,0:T(8,128)S(1)} copy-done((f32[2,16,64,128]{3,2,1,0:T(8,128)S(1)}, f32[2,16,64,128]{3,2,1,0:T(8,128)}, u32[]{:S(2)}) %copy-start) | copy-done | bytes 1048600
  1.9 64.5 %gather_gram.1 = (f32[4,2,16,16,128]{4,3,2,1,0:T(8,128)S(1)}, f32[512,512]{1,0:T(8,128)S(1)}) custom-call(f32[2,16,64,128]{3,2,1,0:T(8,128)S(1)} %copy-done), custom_call_target="tpu_custom_call" | custom-call | tf_op jit(solution)/shard_map/gather_gram/pallas_call | solution.py:364
  66.4 21.5 %factor_core.1 = (f32[512,128]{1,0:T(8,128)}, f32[512,128]{1,0:T(8,128)}) custom-call(f32[4,2,16,16,128]{4,3,2,1,0:T(8,128)S(1)} %get-tuple-element.6.fib, f32[512,512]{1,0:T(8,128)S(1)} %get-tuple-element.7.gram), custom_call_target="tpu_custom_call" | custom-call | tf_op jit(solution)/shard_map/factor_core/pallas_call | solution.py:403
Async XLA Ops:
  0.6 1.2 %copy-start = (f32[2,16,64,128]{3,2,1,0:T(8,128)S(1)}, f32[2,16,64,128]{3,2,1,0:T(8,128)}, u32[]{:S(2)}) copy-start(f32[2,16,64,128]{3,2,1,0:T(8,128)} %field.1) | copy-start | bytes 3145732
where the time goes:
time: 88.1 us; the launch traced here: 87.9 us
  Pallas kernels  86.1 us (98%)
  local copies, waits for them, and re-layouts  1.22 us (1%)
    pallas_call x1, Pallas kernels, on_device(): pl.pallas_call(functools.partial(gather_kernel, sizes, rows * nz * nx * 2...  64.5 us
    pallas_call x1, Pallas kernels, on_device(): pl.pallas_call(factor_kernel, out_shape=(jax.ShapeDtypeStruct((rows, RANK...  21.5 us

commit v1 on v0

--- a/solution.py
+++ b/solution.py
@@ -28,9 +28,13 @@
     return [(i, j) for i in range(blocks) for j in range(i, blocks)]
 
 
+def ring(n, k):
+    return min(k % n, -k % n)
+
+
 def gather_kernel(
-    sizes, total_rows, field, fib, gram, acc, half, core_in, plane_in, mine, z_in, z_sum, plane_all, all_rows,
-    own_sem, a2a_send, a2a_recv, core_send, core_recv, plane_send, plane_recv, z_send, z_recv,
+    sizes, total_rows, field, fib, sums, acc, half, core_in, plane_in, mine, z_in, z_sum,
+    known, own_sem, a2a_send, a2a_recv, core_send, core_recv, plane_send, plane_recv, z_send, z_recv,
     zg_send, zg_recv, pg_send, pg_recv, cg_send, cg_recv,
 ):
     nz, nx, ny = sizes
@@ -49,30 +53,27 @@
     y = lax.axis_index("gz")
     p = x * ny + y
 
-    def peer_plane(k):
-        q = lax.rem(p + k, planes)
-        return q, {"gy": (q // ny) * 2 + c, "gz": lax.rem(q, ny)}
+    def at_x(k):
+        return {"gy": lax.rem(x + k % nx, nx) * 2 + c}
+
+    def at_y(k):
+        return {"gz": lax.rem(y + k % ny, ny)}
+
+    def at_z(k):
+        return {"gx": lax.rem(z + k % nz, nz)}
 
     other = {"gy": x * 2 + (1 - c)}
 
     barrier = pltpu.get_barrier_semaphore()
-    pl.semaphore_signal(barrier, inc=1, device_id=other)
-
-    def greet_plane(k, _):
-        pl.semaphore_signal(barrier, inc=1, device_id=peer_plane(k)[1])
-        return 0
-
-    def greet_z(k, _):
-        pl.semaphore_signal(barrier, inc=1, device_id={"gx": lax.rem(z + k, nz)})
-        return 0
-
-    lax.fori_loop(1, planes, greet_plane, 0)
-    lax.fori_loop(1, nz, greet_z, 0)
-    pl.semaphore_wait(barrier, planes + nz - 1)
+    near = [at_y(k) for k in range(1, ny)] + [other, at_x(1), at_x(-1), at_z(1), at_z(-1)]
+    for device in near:
+        pl.semaphore_signal(barrier, inc=1, device_id=device)
+    pl.semaphore_wait(barrier, len(near))
 
     sends = []
+    order = sorted(range(1, ny), key=lambda k: -ring(ny, k))
     for s in range(steps):
-        for k in range(1, ny):
+        for k in order:
             to = lax.rem(y + k, ny)
             copy = pltpu.make_async_remote_copy(
                 src_ref=field.at[s, :, pl.ds(to * cells, cells), :],
@@ -88,10 +89,19 @@
         copy = pltpu.make_async_copy(field.at[s, :, pl.ds(y * cells, cells), :], fib.at[y, s], own_sem.at[s])
         copy.start()
         owns.append(copy)
+
+    rounds = [[at_x(1), at_x(-1), at_z(1), at_z(-1)], [at_z(2), at_z(-2)], [at_z(4), at_z(-4)]]
+    if nx > 2:
+        rounds[1].append(at_x(2))
+    for i, devices in enumerate(rounds):
+        for device in devices:
+            pl.semaphore_signal(known.at[i], inc=1, device_id=device)
+        pl.semaphore_wait(known.at[i], len(devices))
+
     for s in range(steps):
         owns[s].wait()
-        for k in range(1, ny):
-            sends[s * (ny - 1) + k - 1].wait_recv()
+        for i in range(ny - 1):
+            sends[s * (ny - 1) + i].wait_recv()
         rows = jnp.concatenate([fib[b, s].reshape(-1, LANES) for b in range(blocks)], axis=1)
         for i in range(0, blocks, 2):
             term = full_dot(rows[:, i * LANES : (i + 2) * LANES], rows[:, i * LANES :], 0, 0)
@@ -106,53 +116,46 @@
 
     keep = pl.multiple_of(c * half_rows, 8)
     give = pl.multiple_of((1 - c) * half_rows, 8)
-    copy = pltpu.make_async_remote_copy(
+    core_copy = pltpu.make_async_remote_copy(
         src_ref=acc.at[pl.ds(give, half_rows)],
         dst_ref=core_in,
         send_sem=core_send,
         recv_sem=core_recv,
         device_id=other,
     )
-    copy.start()
-    copy.wait_recv()
+    core_copy.start()
+    core_copy.wait_recv()
     half[...] = acc[pl.ds(keep, half_rows), :] + core_in[...]
-    copy.wait_send()
-
-    def plane_copy(k):
-        q, device = peer_plane(k)
-        return pltpu.make_async_remote_copy(
+
+    offsets = [(i, j) for i in range(nx) for j in range(ny) if (i, j) != (0, 0)]
+    offsets.sort(key=lambda o: -(ring(nx, o[0]) + ring(ny, o[1])))
+
+    def plane_at(i, j):
+        to_x, to_y = lax.rem(x + i % nx, nx), lax.rem(y + j % ny, ny)
+        return to_x * ny + to_y, {"gy": to_x * 2 + c, "gz": to_y}
+
+    plane_copies = []
+    for n, (i, j) in enumerate(offsets):
+        q, device = plane_at(i, j)
+        copy = pltpu.make_async_remote_copy(
             src_ref=half.at[pl.ds(pl.multiple_of(q * piece, 8), piece)],
-            dst_ref=plane_in.at[k - 1],
-            send_sem=plane_send.at[k - 1],
-            recv_sem=plane_recv.at[k - 1],
+            dst_ref=plane_in.at[n],
+            send_sem=plane_send.at[n],
+            recv_sem=plane_recv.at[n],
             device_id=device,
         )
-
-    def start(make):
-        def body(k, _):
-            make(k).start()
-            return 0
-
-        return body
-
-    def finish(make):
-        def body(k, _):
-            make(k).wait_send()
-            return 0
-
-        return body
-
-    lax.fori_loop(1, planes, start(plane_copy), 0)
-
-    def plane_add(k, total):
-        plane_copy(k).wait_recv()
-        return total + plane_in[k - 1]
-
-    mine[...] = lax.fori_loop(1, planes, plane_add, half[pl.ds(pl.multiple_of(p * piece, 8), piece), :])
+        copy.start()
+        plane_copies.append(copy)
+    total = half[pl.ds(pl.multiple_of(p * piece, 8), piece), :]
+    for n in reversed(range(len(offsets))):
+        plane_copies[n].wait_recv()
+        total = total + plane_in[n]
+    mine[...] = total
 
     spread = nz // tiles
     tile = lax.rem(z // spread, tiles)
     owner = (lax.rem(z, spread) == 0) & (z // spread < tiles)
+    distances = sorted(range(1, nz), key=lambda k: -ring(nz, k))
 
     def z_copy(t):
         return pltpu.make_async_remote_copy(
@@ -163,6 +166,15 @@
             device_id={"gx": t * spread},
         )
 
+    def zg_copy(i, t):
+        return pltpu.make_async_remote_copy(
+            src_ref=z_sum.at[t],
+            dst_ref=z_sum.at[t],
+            send_sem=zg_send.at[i],
+            recv_sem=zg_recv.at[t],
+            device_id=at_z(distances[i]),
+        )
+
     for t in range(tiles):
 
         @pl.when(z != t * spread)
@@ -171,7 +183,8 @@
 
     @pl.when(owner)
     def _():
-        def z_add(k, total):
+        total = mine[pl.ds(pl.multiple_of(tile * 8, 8), 8), :]
+        for k in reversed(distances):
             w = lax.rem(z + k, nz)
             pltpu.make_async_remote_copy(
                 src_ref=z_in.at[w],
@@ -180,90 +193,49 @@
                 recv_sem=z_recv.at[w],
                 device_id={"gx": w},
             ).wait_recv()
-            return total + z_in[w]
-
-        own = mine[pl.ds(pl.multiple_of(tile * 8, 8), 8), :]
-        z_sum[tile] = lax.fori_loop(1, nz, z_add, own) * jnp.float32(1.0 / total_rows)
-
-    def zg_copy(k):
-        return pltpu.make_async_remote_copy(
-            src_ref=z_sum.at[tile],
-            dst_ref=z_sum.at[tile],
-            send_sem=zg_send.at[k - 1],
-            recv_sem=zg_recv.at[tile],
-            device_id={"gx": lax.rem(z + k, nz)},
-        )
-
-    @pl.when(owner)
-    def _():
-        lax.fori_loop(1, nz, start(zg_copy), 0)
+            total = total + z_in[w]
+        z_sum[tile] = total * jnp.float32(1.0 / total_rows)
+        for i in range(nz - 1):
+            zg_copy(i, tile).start()
 
     for t in range(tiles):
 
         @pl.when(z != t * spread)
         def _():
-            pltpu.make_async_remote_copy(
-                src_ref=z_sum.at[t],
-                dst_ref=z_sum.at[t],
-                send_sem=zg_send.at[0],
-                recv_sem=zg_recv.at[t],
-                device_id={"gx": lax.rem(z + 1, nz)},
-            ).wait_recv()
-
-    plane_all[p] = z_sum[...].reshape(piece, LANES)
-
-    def pg_copy(k):
+            zg_copy(0, t).wait_recv()
+
+    sums[c, p] = z_sum[...].reshape(piece, LANES)
+
+    def cg_copy(n, q):
         return pltpu.make_async_remote_copy(
-            src_ref=plane_all.at[p],
-            dst_ref=plane_all.at[p],
-            send_sem=pg_send.at[k - 1],
-            recv_sem=pg_recv.at[k - 1],
-            device_id=peer_plane(k)[1],
-        )
-
-    def cg_copy(k):
-        q = lax.rem(p + planes - k, planes)
-        return pltpu.make_async_remote_copy(
-            src_ref=plane_all.at[q],
-            dst_ref=all_rows.at[q],
-            send_sem=cg_send.at[k],
-            recv_sem=cg_recv.at[k],
+            src_ref=sums.at[c, q],
+            dst_ref=sums.at[c, q],
+            send_sem=cg_send.at[n],
+            recv_sem=cg_recv.at[n],
             device_id=other,
         )
 
-    lax.fori_loop(1, planes, start(pg_copy), 0)
-    cg_copy(0).start()
-
-    def forward(k, _):
-        pg_copy(k).wait_recv()
-        cg_copy(k).start()
-        return 0
-
-    lax.fori_loop(1, planes, forward, 0)
-
-    def arrived(k, _):
-        cg_copy(k).wait_recv()
-        return 0
-
-    lax.fori_loop(0, planes, arrived, 0)
-
-    def put(n, block):
-        i, j = pairs[n]
-        gram[i * LANES : (i + 1) * LANES, j * LANES : (j + 1) * LANES] = block
-        if i != j:
-            gram[j * LANES : (j + 1) * LANES, i * LANES : (i + 1) * LANES] = block.T
-
-    here = plane_all[...].reshape(half_rows, LANES)
-    there = all_rows[...].reshape(half_rows, LANES)
-    low = jnp.where(c == 0, here, there)
-    high = jnp.where(c == 0, there, here)
-    both = jnp.concatenate([low, high], axis=0)
-    for n in range(len(pairs)):
-        put(n, both[n * LANES : (n + 1) * LANES, :])
-
-    for copy in sends:
+    pg_copies, cg_copies = [], []
+    for n, (i, j) in enumerate(offsets):
+        copy = pltpu.make_async_remote_copy(
+            src_ref=sums.at[c, p],
+            dst_ref=sums.at[c, p],
+            send_sem=pg_send.at[n],
+            recv_sem=pg_recv.at[n],
+            device_id=plane_at(i, j)[1],
+        )
+        copy.start()
+        pg_copies.append(copy)
+    cg_copies.append(cg_copy(len(offsets), p))
+    cg_copies[-1].start()
+    for n in reversed(range(len(offsets))):
+        i, j = offsets[n]
+        pg_copies[n].wait_recv()
+        cg_copies.append(cg_copy(n, plane_at(-i, -j)[0]))
+        cg_copies[-1].start()
+
+    for copy in sends + [core_copy] + plane_copies + pg_copies:
         copy.wait_send()
-    lax.fori_loop(1, planes, finish(plane_copy), 0)
     for t in range(tiles):
 
         @pl.when(z != t * spread)
@@ -272,10 +244,11 @@
 
     @pl.when(owner)
     def _():
-        lax.fori_loop(1, nz, finish(zg_copy), 0)
-
-    lax.fori_loop(1, planes, finish(pg_copy), 0)
-    lax.fori_loop(0, planes, finish(cg_copy), 0)
+        for i in range(nz - 1):
+            zg_copy(i, tile).wait_send()
+
+    for copy in cg_copies:
+        copy.wait()
 
 
 def reciprocal(d):
@@ -332,19 +305,27 @@
             w[j1:, :] = w[j1:, :] - full_dot(upper[:, j1:rank], upper, 0, 0)
 
 
-def factor_kernel(fib, gram, core, factor, w, factor_t):
+def factor_kernel(fib, sums, core, factor, gram, w, factor_t):
     rank = w.shape[0]
+    blocks = fib.shape[0]
+    pairs = block_pairs(blocks)
+    part = [sums[n * LANES : (n + 1) * LANES, :] for n in range(len(pairs))]
     for step in range(ITERS):
         if step == 0:
-            grown_t = gram[:rank, :]
+            grown_t = jnp.concatenate(part[:blocks], axis=1)
         else:
             grown_t = full_dot(factor_t[...], gram[...], 1, 0)
         w[:, rank:] = grown_t
         w[:, :rank] = full_dot(grown_t, grown_t, 1, 1)
         eliminate(w, factor_t)
+        if step == 0:
+            for n, (i, j) in enumerate(pairs):
+                gram[i * LANES : (i + 1) * LANES, j * LANES : (j + 1) * LANES] = part[n]
+                if i != j:
+                    gram[j * LANES : (j + 1) * LANES, i * LANES : (i + 1) * LANES] = part[n].T
     result = factor_t[...].T
     factor[...] = result
-    rows = jnp.concatenate([fib[b].reshape(-1, LANES) for b in range(fib.shape[0])], axis=1)
+    rows = jnp.concatenate([fib[b].reshape(-1, LANES) for b in range(blocks)], axis=1)
     core[...] = full_dot(rows, result, 1, 0)
 
 
@@ -361,11 +342,11 @@
     tiles = piece // 8
     f32 = jnp.float32
     dma = pltpu.SemaphoreType.DMA
-    fib, gram = pl.pallas_call(
+    fib, sums = pl.pallas_call(
         functools.partial(gather_kernel, sizes, rows * nz * nx * 2 * ny),
         out_shape=(
             jax.ShapeDtypeStruct((ny, steps, width_x, cells, width_z), f32),
-            jax.ShapeDtypeStruct((width, width), f32),
+            jax.ShapeDtypeStruct((2, planes, piece, LANES), f32),
         ),
         in_specs=[pl.BlockSpec(memory_space=pl.ANY)],
         out_specs=(VMEM, VMEM),
@@ -377,8 +358,7 @@
             pltpu.VMEM((piece, LANES), f32),
             pltpu.VMEM((nz, 8, LANES), f32),
             pltpu.VMEM((tiles, 8, LANES), f32),
-            pltpu.VMEM((planes, piece, LANES), f32),
-            pltpu.VMEM((planes, piece, LANES), f32),
+            pltpu.SemaphoreType.REGULAR((3,)),
             dma((steps,)),
             dma((steps, ny - 1)),
             dma((steps, ny - 1)),
@@ -409,12 +389,13 @@
         in_specs=[VMEM, VMEM],
         out_specs=(VMEM, VMEM),
         scratch_shapes=[
+            pltpu.VMEM((width, width), f32),
             pltpu.VMEM((RANK, RANK + width), f32),
             pltpu.VMEM((RANK, width), f32),
         ],
         compiler_params=pltpu.CompilerParams(vmem_limit_bytes=24 * 2**20),
         name="factor_core",
-    )(fib, gram)
+    )(fib, sums.reshape(pair_rows, LANES))
     return core.reshape(steps, width_x, cells, RANK), factor
 
 

time: 88.1 us -> 80.1 us (0.909)
  Pallas kernels: 86.1 us -> 78.1 us
    pallas_call x1, Pallas kernels: 64.5 us -> 56.8 us  [on_device(): pl.pallas_call(functools.partial(gather_kernel, sizes, rows * nz * nx * 2...]
where the time goes in v1:
time: 80.1 us; the launch traced here: 80 us
  Pallas kernels  78.1 us (98%)
  local copies, waits for them, and re-layouts  1.22 us (2%)
    pallas_call x1, Pallas kernels, on_device(): pl.pallas_call(functools.partial(gather_kernel, sizes, rows * nz * nx * 2...  56.8 us
    pallas_call x1, Pallas kernels, on_device(): pl.pallas_call(factor_kernel, out_shape=(jax.ShapeDtypeStruct((rows, RANK...  21.3 us

profile of v1, /device:TPU:1, one launch (start us, length us, event | category | flops | bytes accessed | tf_op | source)
XLA Modules:
  0.0 80.0 jit_solution(11835829372065113444)
XLA Ops:
  0.6 0.0 copy-start
  0.6 1.2 %copy-done = f32[2,16,64,128]{3,2,1,0:T(8,128)S(1)} copy-done((f32[2,16,64,128]{3,2,1,0:T(8,128)S(1)}, f32[2,16,64,128]{3,2,1,0:T(8,128)}, u32[]{:S(2)}) %copy-start) | copy-done | bytes 1048600
  1.9 56.8 %gather_gram.1 = (f32[4,2,16,16,128]{4,3,2,1,0:T(8,128)S(1)}, f32[2,16,40,128]{3,2,1,0:T(8,128)S(1)}) custom-call(f32[2,16,64,128]{3,2,1,0:T(8,128)S(1)} %copy-done), custom_call_target="tpu_custom_call" | custom-call | tf_op jit(solution)/shard_map/gather_gram/pallas_call | solution.py:345
  58.7 21.3 %factor_core.1 = (f32[512,128]{1,0:T(8,128)}, f32[512,128]{1,0:T(8,128)}) custom-call(f32[4,2,16,16,128]{4,3,2,1,0:T(8,128)S(1)} %get-tuple-element.6.fib, f32[1280,128]{1,0:T(8,128)S(1)} %bitcast.2), custom_call_target="tpu_custom_call" | custom-call | tf_op jit(solution)/shard_map/factor_core/pallas_call | solution.py:383
Async XLA Ops:
  0.6 1.2 %copy-start = (f32[2,16,64,128]{3,2,1,0:T(8,128)S(1)}, f32[2,16,64,128]{3,2,1,0:T(8,128)}, u32[]{:S(2)}) copy-start(f32[2,16,64,128]{3,2,1,0:T(8,128)} %field.1) | copy-start | bytes 3145732

commit v2 on v1

--- a/solution.py
+++ b/solution.py
@@ -11,6 +11,7 @@
 ITERS = 4
 LANES = 128
 PANEL = 32
+BLOCK = 16
 VMEM = pl.BlockSpec(memory_space=pltpu.VMEM)
 
 
@@ -256,77 +257,129 @@
     return r * (2.0 - d * r)
 
 
-def eliminate(w, factor_t):
-    wide = w.shape[1]
-    rank = w.shape[0]
-    groups = PANEL // 8
-    rows = lax.broadcasted_iota(jnp.int32, (8, LANES), 0)
-
-    def spread(v):
-        return jnp.concatenate([v] * (wide // LANES), axis=1)
-
-    def row(v, i):
-        return jnp.broadcast_to(v[i : i + 1, :], (8, v.shape[1]))
-
-    for j0 in range(0, rank, PANEL):
-        panel = [w[j0 + 8 * g : j0 + 8 * g + 8, :] for g in range(groups)]
-        cols = {}
-        for k in range(PANEL):
-            for g in range(k // 8, groups):
-                cols[k, g] = jnp.broadcast_to(panel[g][:, j0 + k : j0 + k + 1], (8, LANES))
-        scale = [jnp.ones((8, LANES), jnp.float32) for _ in range(groups)]
-        for j in range(PANEL):
-            gj, ij = j // 8, j % 8
-            pivot = row(cols[j, gj], ij)
-            inverse = reciprocal(pivot)
-            if j + 1 < PANEL:
-                k = j + 1
-                across = row(cols[j, k // 8], k % 8)
-                for g in range(k // 8, groups):
-                    cols[k, g] = cols[k, g] - (cols[j, g] * across) * inverse
-            multiplier = {g: cols[j, g] * inverse for g in range(gj, groups)}
-            for k in range(j + 2, PANEL):
-                across = row(cols[j, k // 8], k % 8)
-                for g in range(k // 8, groups):
-                    cols[k, g] = cols[k, g] - multiplier[g] * across
-            pivot_row = row(panel[gj], ij)
-            scale[gj] = jnp.where(rows == ij, lax.rsqrt(pivot), scale[gj])
-            for g in range(gj, groups):
-                if g > gj:
-                    panel[g] = panel[g] - spread(multiplier[g]) * pivot_row
-                elif ij < 7:
-                    panel[g] = panel[g] - spread(jnp.where(rows > ij, multiplier[g], 0.0)) * pivot_row
-        panel = [panel[g] * spread(scale[g]) for g in range(groups)]
+def short_dot(a, b, ca, cb):
+    return lax.dot_general(a, b, (((ca,), (cb,)), ((), ())), preferred_element_type=jnp.float32)
+
+
+def split(v):
+    high = v.astype(jnp.bfloat16)
+    rest = v - high.astype(jnp.float32)
+    middle = rest.astype(jnp.bfloat16)
+    return high, middle, (rest - middle.astype(jnp.float32)).astype(jnp.bfloat16)
+
+
+def left(v, axis):
+    h, m, t = split(v)
+    return jnp.concatenate([h, h, m, m, h, t], axis=axis)
+
+
+def right(v, axis):
+    h, m, t = split(v)
+    return jnp.concatenate([h, m, h, m, t, h], axis=axis)
+
+
+def row(v, i):
+    return jnp.broadcast_to(v[i : i + 1, :], (8, v.shape[1]))
+
+
+def inverse_lower(inner):
+    rank = inner.shape[0]
+    count, groups = rank // PANEL, PANEL // 8
+    row8 = lax.broadcasted_iota(jnp.int32, (8, rank), 0)
+    lane8 = lax.broadcasted_iota(jnp.int32, (8, rank), 1)
+    row_of = lax.broadcasted_iota(jnp.int32, (PANEL, rank), 0)
+    lane_of = lax.broadcasted_iota(jnp.int32, (PANEL, rank), 1)
+    rest = [inner[t * PANEL : (t + 1) * PANEL] for t in range(count)]
+    result = []
+    for s in range(count):
+        j0, j1 = s * PANEL, (s + 1) * PANEL
+        panel = [rest[s][8 * g : 8 * g + 8, :] for g in range(groups)]
+        done = {}
+        for g0 in range(0, groups, BLOCK // 8):
+            c0 = j0 + 8 * g0
+            cols = {}
+            for k in range(BLOCK):
+                for g in range(g0 + k // 8, groups):
+                    cols[k, g] = jnp.broadcast_to(panel[g][:, c0 + k : c0 + k + 1], (8, rank))
+
+            def at(j, k):
+                return row(cols[j, g0 + k // 8], k % 8)
+
+            p, q, r = at(0, 0), at(0, 1), at(1, 1)
+            for j in range(0, BLOCK, 2):
+                gj, ij = g0 + j // 8, j % 8
+                column = c0 + j
+                det = p * r - q * q
+                inv = reciprocal(det)
+                following = None
+                if j + 2 < BLOCK:
+                    k = j + 2
+                    u1, u2, v1, v2 = at(j, k), at(j + 1, k), at(j, k + 1), at(j + 1, k + 1)
+                    a1, a2 = r * u1 - q * u2, p * u2 - q * u1
+                    e1, e2 = r * v1 - q * v2, p * v2 - q * v1
+                    following = (
+                        at(k, k) - (a1 * u1 + a2 * u2) * inv,
+                        at(k, k + 1) - (a1 * v1 + a2 * v2) * inv,
+                        at(k + 1, k + 1) - (e1 * v1 + e2 * v2) * inv,
+                    )
+                pi, qi, ri = p * inv, q * inv, r * inv
+                first = gj + 1 if ij == 6 else gj
+                m1 = {g: cols[j, g] * ri - cols[j + 1, g] * qi for g in range(first, groups)}
+                m2 = {g: cols[j + 1, g] * pi - cols[j, g] * qi for g in range(first, groups)}
+                for k in range(j + 2, BLOCK):
+                    w1, w2 = at(j, k), at(j + 1, k)
+                    for g in range(g0 + k // 8, groups):
+                        cols[k, g] = cols[k, g] - (m1[g] * w1 + m2[g] * w2)
+                here = lane8 // 2 == column // 2
+                row1 = jnp.where(here, jnp.where(lane8 == column, 1.0, 0.0), row(panel[gj], ij))
+                row2 = jnp.where(here, jnp.where(lane8 == column, 0.0, 1.0), row(panel[gj], ij + 1))
+                inv_p = reciprocal(p)
+                done[8 * gj + ij] = row1 * lax.rsqrt(p)
+                done[8 * gj + ij + 1] = (row2 - (q * inv_p) * row1) * lax.rsqrt(det * inv_p)
+                for g in range(first, groups):
+                    panel[g] = jnp.where(here, 0.0, panel[g]) - (m1[g] * row1 + m2[g] * row2)
+                if following:
+                    p, q, r = following
+        upper = []
         for g in range(groups):
-            factor_t[j0 + 8 * g : j0 + 8 * g + 8, :] = panel[g][:, rank:]
-        j1 = j0 + PANEL
-        if j1 < rank:
-            upper = jnp.concatenate(panel, axis=0)
-            w[j1:, :] = w[j1:, :] - full_dot(upper[:, j1:rank], upper, 0, 0)
-
-
-def factor_kernel(fib, sums, core, factor, gram, w, factor_t):
-    rank = w.shape[0]
+            v = done[8 * g]
+            for i in range(1, 8):
+                v = jnp.where(row8 == i, done[8 * g + i], v)
+            upper.append(v)
+        upper = jnp.concatenate(upper, axis=0)
+        lower = lane_of <= row_of + j0
+        result.append(jnp.where(lower, upper, 0.0))
+        if s + 1 < count:
+            kept = jnp.where(lower | (lane_of >= j1), upper, 0.0)
+            change = short_dot(left(upper, 0)[:, j1:], right(kept, 0), 0, 0)
+            block = (lane_of >= j0) & (lane_of < j1)
+            for t in range(s + 1, count):
+                part = change[(t - s - 1) * PANEL : (t - s) * PANEL]
+                rest[t] = jnp.where(block, 0.0, rest[t]) - part
+    return jnp.concatenate(result, axis=0)
+
+
+def factor_kernel(fib, sums, core, factor, gram):
     blocks = fib.shape[0]
+    width = blocks * LANES
     pairs = block_pairs(blocks)
     part = [sums[n * LANES : (n + 1) * LANES, :] for n in range(len(pairs))]
+    for n, (i, j) in enumerate(pairs):
+        gram[i * LANES : (i + 1) * LANES, j * LANES : (j + 1) * LANES] = part[n]
+        if i != j:
+            gram[j * LANES : (j + 1) * LANES, i * LANES : (i + 1) * LANES] = part[n].T
+    grown_t = jnp.concatenate(part[:blocks], axis=1)
     for step in range(ITERS):
-        if step == 0:
-            grown_t = jnp.concatenate(part[:blocks], axis=1)
+        inner = full_dot(grown_t, grown_t, 1, 1)
+        if step < ITERS - 1:
+            ready = right(full_dot(grown_t, gram[...], 1, 0), 0)
+            grown_t = short_dot(left(inverse_lower(inner), 1), ready, 1, 0)
         else:
-            grown_t = full_dot(factor_t[...], gram[...], 1, 0)
-        w[:, rank:] = grown_t
-        w[:, :rank] = full_dot(grown_t, grown_t, 1, 1)
-        eliminate(w, factor_t)
-        if step == 0:
-            for n, (i, j) in enumerate(pairs):
-                gram[i * LANES : (i + 1) * LANES, j * LANES : (j + 1) * LANES] = part[n]
-                if i != j:
-                    gram[j * LANES : (j + 1) * LANES, i * LANES : (i + 1) * LANES] = part[n].T
-    result = factor_t[...].T
-    factor[...] = result
-    rows = jnp.concatenate([fib[b].reshape(-1, LANES) for b in range(blocks)], axis=1)
-    core[...] = full_dot(rows, result, 1, 0)
+            rows = jnp.concatenate([fib[b].reshape(-1, LANES) for b in range(blocks)], axis=1)
+            ready = left(jnp.concatenate([grown_t.T, full_dot(rows, grown_t, 1, 1)], axis=0), 1)
+            both = short_dot(ready, right(inverse_lower(inner), 1), 1, 1)
+            factor[...] = both[:width]
+            core[...] = both[width:]
 
 
 def on_device(sizes, field):
@@ -390,8 +443,6 @@
         out_specs=(VMEM, VMEM),
         scratch_shapes=[
             pltpu.VMEM((width, width), f32),
-            pltpu.VMEM((RANK, RANK + width), f32),
-            pltpu.VMEM((RANK, width), f32),
         ],
         compiler_params=pltpu.CompilerParams(vmem_limit_bytes=24 * 2**20),
         name="factor_core",

time: 80.1 us -> 75.7 us (0.945)
  Pallas kernels: 78.1 us -> 73.7 us
    pallas_call x1, Pallas kernels: 21.3 us -> 16.9 us  [on_device(): pl.pallas_call(factor_kernel, out_shape=(jax.ShapeDtypeStruct((rows, RANK...]
where the time goes in v2:
time: 75.7 us; the launch traced here: 75.5 us
  Pallas kernels  73.7 us (97%)
  local copies, waits for them, and re-layouts  1.22 us (2%)
    pallas_call x1, Pallas kernels, on_device(): pl.pallas_call(functools.partial(gather_kernel, sizes, rows * nz * nx * 2...  56.8 us
    pallas_call x1, Pallas kernels, on_device(): pl.pallas_call(factor_kernel, out_shape=(jax.ShapeDtypeStruct((rows, RANK...  16.9 us

profile of v2, /device:TPU:1, one launch (start us, length us, event | category | flops | bytes accessed | tf_op | source)
XLA Modules:
  0.0 75.5 jit_solution(12335713542588433758)
XLA Ops:
  0.6 0.0 copy-start
  0.6 1.2 %copy-done = f32[2,16,64,128]{3,2,1,0:T(8,128)S(1)} copy-done((f32[2,16,64,128]{3,2,1,0:T(8,128)S(1)}, f32[2,16,64,128]{3,2,1,0:T(8,128)}, u32[]{:S(2)}) %copy-start) | copy-done | bytes 1048600
  1.9 56.8 %gather_gram.1 = (f32[4,2,16,16,128]{4,3,2,1,0:T(8,128)S(1)}, f32[2,16,40,128]{3,2,1,0:T(8,128)S(1)}) custom-call(f32[2,16,64,128]{3,2,1,0:T(8,128)S(1)} %copy-done), custom_call_target="tpu_custom_call" | custom-call | tf_op jit(solution)/shard_map/gather_gram/pallas_call | solution.py:398
  58.7 16.9 %factor_core.1 = (f32[512,128]{1,0:T(8,128)}, f32[512,128]{1,0:T(8,128)}) custom-call(f32[4,2,16,16,128]{4,3,2,1,0:T(8,128)S(1)} %get-tuple-element.6.fib, f32[1280,128]{1,0:T(8,128)S(1)} %bitcast.2), custom_call_target="tpu_custom_call" | custom-call | tf_op jit(solution)/shard_map/factor_core/pallas_call | solution.py:436
Async XLA Ops:
  0.6 1.2 %copy-start = (f32[2,16,64,128]{3,2,1,0:T(8,128)S(1)}, f32[2,16,64,128]{3,2,1,0:T(8,128)}, u32[]{:S(2)}) copy-start(f32[2,16,64,128]{3,2,1,0:T(8,128)} %field.1) | copy-start | bytes 3145732

commit v3 on v2

--- a/solution.py
+++ b/solution.py
@@ -71,23 +71,27 @@
         pl.semaphore_signal(barrier, inc=1, device_id=device)
     pl.semaphore_wait(barrier, len(near))
 
+    deep = fib.shape[2] // 2
+    chunks = [(s, pl.ds(h * deep, deep)) for s in range(steps) for h in range(2)]
     sends = []
     order = sorted(range(1, ny), key=lambda k: -ring(ny, k))
-    for s in range(steps):
+    for n, (s, part) in enumerate(chunks):
         for k in order:
             to = lax.rem(y + k, ny)
             copy = pltpu.make_async_remote_copy(
-                src_ref=field.at[s, :, pl.ds(to * cells, cells), :],
-                dst_ref=fib.at[y, s],
-                send_sem=a2a_send.at[s, k - 1],
-                recv_sem=a2a_recv.at[s, k - 1],
+                src_ref=field.at[s, part, pl.ds(to * cells, cells), :],
+                dst_ref=fib.at[y, s, part],
+                send_sem=a2a_send.at[n, k - 1],
+                recv_sem=a2a_recv.at[n, k - 1],
                 device_id={"gz": to},
             )
             copy.start()
             sends.append(copy)
     owns = []
-    for s in range(steps):
-        copy = pltpu.make_async_copy(field.at[s, :, pl.ds(y * cells, cells), :], fib.at[y, s], own_sem.at[s])
+    for n, (s, part) in enumerate(chunks):
+        copy = pltpu.make_async_copy(
+            field.at[s, part, pl.ds(y * cells, cells), :], fib.at[y, s, part], own_sem.at[n]
+        )
         copy.start()
         owns.append(copy)
 
@@ -99,34 +103,22 @@
             pl.semaphore_signal(known.at[i], inc=1, device_id=device)
         pl.semaphore_wait(known.at[i], len(devices))
 
-    for s in range(steps):
-        owns[s].wait()
+    for n, (s, _) in enumerate(chunks):
+        owns[n].wait()
         for i in range(ny - 1):
-            sends[s * (ny - 1) + i].wait_recv()
-        rows = jnp.concatenate([fib[b, s].reshape(-1, LANES) for b in range(blocks)], axis=1)
+            sends[n * (ny - 1) + i].wait_recv()
+        x0 = (n % 2) * deep
+        rows = jnp.concatenate([fib[b, s, x0 : x0 + deep].reshape(-1, LANES) for b in range(blocks)], axis=1)
         for i in range(0, blocks, 2):
             term = full_dot(rows[:, i * LANES : (i + 2) * LANES], rows[:, i * LANES :], 0, 0)
             for a in (0, 1):
                 for b in range(i + a, blocks):
-                    n = pairs.index((i + a, b)) * LANES
+                    r = pairs.index((i + a, b)) * LANES
                     part = term[a * LANES : (a + 1) * LANES, (b - i) * LANES : (b - i + 1) * LANES]
-                    if s == 0:
-                        acc[n : n + LANES, :] = part
+                    if n == 0:
+                        acc[r : r + LANES, :] = part
                     else:
-                        acc[n : n + LANES, :] = acc[n : n + LANES, :] + part
-
-    keep = pl.multiple_of(c * half_rows, 8)
-    give = pl.multiple_of((1 - c) * half_rows, 8)
-    core_copy = pltpu.make_async_remote_copy(
-        src_ref=acc.at[pl.ds(give, half_rows)],
-        dst_ref=core_in,
-        send_sem=core_send,
-        recv_sem=core_recv,
-        device_id=other,
-    )
-    core_copy.start()
-    core_copy.wait_recv()
-    half[...] = acc[pl.ds(keep, half_rows), :] + core_in[...]
+                        acc[r : r + LANES, :] = acc[r : r + LANES, :] + part
 
     offsets = [(i, j) for i in range(nx) for j in range(ny) if (i, j) != (0, 0)]
     offsets.sort(key=lambda o: -(ring(nx, o[0]) + ring(ny, o[1])))
@@ -135,11 +127,30 @@
         to_x, to_y = lax.rem(x + i % nx, nx), lax.rem(y + j % ny, ny)
         return to_x * ny + to_y, {"gy": to_x * 2 + c, "gz": to_y}
 
+    def rows_of(start, q):
+        return pl.ds(pl.multiple_of(start + q * piece, 8), piece)
+
+    keep = c * half_rows
+    give = (1 - c) * half_rows
+    core_copies = []
+    for n, (i, j) in enumerate(offsets + [(0, 0)]):
+        q = plane_at(i, j)[0]
+        copy = pltpu.make_async_remote_copy(
+            src_ref=acc.at[rows_of(give, q)],
+            dst_ref=core_in.at[rows_of(0, q)],
+            send_sem=core_send.at[n],
+            recv_sem=core_recv.at[n],
+            device_id=other,
+        )
+        copy.start()
+        core_copies.append(copy)
     plane_copies = []
     for n, (i, j) in enumerate(offsets):
         q, device = plane_at(i, j)
+        core_copies[n].wait_recv()
+        half[rows_of(0, q), :] = acc[rows_of(keep, q), :] + core_in[rows_of(0, q), :]
         copy = pltpu.make_async_remote_copy(
-            src_ref=half.at[pl.ds(pl.multiple_of(q * piece, 8), piece)],
+            src_ref=half.at[rows_of(0, q)],
             dst_ref=plane_in.at[n],
             send_sem=plane_send.at[n],
             recv_sem=plane_recv.at[n],
@@ -147,24 +158,29 @@
         )
         copy.start()
         plane_copies.append(copy)
-    total = half[pl.ds(pl.multiple_of(p * piece, 8), piece), :]
+    core_copies[-1].wait_recv()
+    total = acc[rows_of(keep, p), :] + core_in[rows_of(0, p), :]
     for n in reversed(range(len(offsets))):
         plane_copies[n].wait_recv()
         total = total + plane_in[n]
     mine[...] = total
 
     spread = nz // tiles
-    tile = lax.rem(z // spread, tiles)
-    owner = (lax.rem(z, spread) == 0) & (z // spread < tiles)
-    distances = sorted(range(1, nz), key=lambda k: -ring(nz, k))
-
-    def z_copy(t):
+    keepers = [(t * spread % nz, (t * spread + nz // 2) % nz) for t in range(tiles)]
+    assert len({v for pair in keepers for v in pair}) == 2 * tiles
+    reach = sorted((k for k in range(1 - nz // 4, nz // 4 + 1) if k), key=lambda k: -ring(nz, k))
+    distances = sorted(range(1, nz), key=lambda k: ring(nz, k))
+    keeps = [(z == a) | (z == b) for a, b in keepers]
+    keeper = functools.reduce(lambda v, w: v | w, keeps)
+    tile = sum(t * keeps[t].astype(jnp.int32) for t in range(tiles))
+
+    def z_copy(t, m):
         return pltpu.make_async_remote_copy(
             src_ref=mine.at[pl.ds(t * 8, 8)],
             dst_ref=z_in.at[z],
-            send_sem=z_send.at[t],
+            send_sem=z_send.at[t, m],
             recv_sem=z_recv.at[z],
-            device_id={"gx": t * spread},
+            device_id={"gx": keepers[t][m]},
         )
 
     def zg_copy(i, t):
@@ -173,35 +189,38 @@
             dst_ref=z_sum.at[t],
             send_sem=zg_send.at[i],
             recv_sem=zg_recv.at[t],
-            device_id=at_z(distances[i]),
+            device_id=at_z(reach[i]),
         )
 
     for t in range(tiles):
-
-        @pl.when(z != t * spread)
-        def _():
-            z_copy(t).start()
-
-    @pl.when(owner)
+        for m in (0, 1):
+
+            @pl.when(z != keepers[t][m])
+            def _():
+                z_copy(t, m).start()
+
+    @pl.when(keeper)
     def _():
-        total = mine[pl.ds(pl.multiple_of(tile * 8, 8), 8), :]
-        for k in reversed(distances):
+        z_in[z] = mine[pl.ds(pl.multiple_of(tile * 8, 8), 8), :]
+        for k in distances:
             w = lax.rem(z + k, nz)
             pltpu.make_async_remote_copy(
                 src_ref=z_in.at[w],
                 dst_ref=z_in.at[w],
-                send_sem=z_send.at[0],
+                send_sem=z_send.at[0, 0],
                 recv_sem=z_recv.at[w],
                 device_id={"gx": w},
             ).wait_recv()
+        total = z_in[0]
+        for w in range(1, nz):
             total = total + z_in[w]
         z_sum[tile] = total * jnp.float32(1.0 / total_rows)
-        for i in range(nz - 1):
+        for i in range(len(reach)):
             zg_copy(i, tile).start()
 
     for t in range(tiles):
 
-        @pl.when(z != t * spread)
+        @pl.when(jnp.logical_not(keeps[t]))
         def _():
             zg_copy(0, t).wait_recv()
 
@@ -235,17 +254,18 @@
         cg_copies.append(cg_copy(n, plane_at(-i, -j)[0]))
         cg_copies[-1].start()
 
-    for copy in sends + [core_copy] + plane_copies + pg_copies:
+    for copy in sends + core_copies + plane_copies + pg_copies:
         copy.wait_send()
     for t in range(tiles):
-
-        @pl.when(z != t * spread)
-        def _():
-            z_copy(t).wait_send()
-
-    @pl.when(owner)
+        for m in (0, 1):
+
+            @pl.when(z != keepers[t][m])
+            def _():
+                z_copy(t, m).wait_send()
+
+    @pl.when(keeper)
     def _():
-        for i in range(nz - 1):
+        for i in range(len(reach)):
             zg_copy(i, tile).wait_send()
 
     for copy in cg_copies:
@@ -412,16 +432,16 @@
             pltpu.VMEM((nz, 8, LANES), f32),
             pltpu.VMEM((tiles, 8, LANES), f32),
             pltpu.SemaphoreType.REGULAR((3,)),
-            dma((steps,)),
-            dma((steps, ny - 1)),
-            dma((steps, ny - 1)),
-            dma,
-            dma,
+            dma((2*steps,)),
+            dma((2*steps, ny - 1)),
+            dma((2*steps, ny - 1)),
+            dma((planes,)),
+            dma((planes,)),
             dma((planes - 1,)),
             dma((planes - 1,)),
-            dma((tiles,)),
+            dma((tiles, 2)),
             dma((nz,)),
-            dma((nz - 1,)),
+            dma((nz // 2 - 1,)),
             dma((tiles,)),
             dma((planes - 1,)),
             dma((planes - 1,)),

time: 75.7 us -> 73.8 us (0.975)
  Pallas kernels: 73.7 us -> 71.8 us
    pallas_call x1, Pallas kernels: 56.8 us -> 54.9 us  [on_device(): pl.pallas_call(functools.partial(gather_kernel, sizes, rows * nz * nx * 2...]
where the time goes in v3:
time: 73.8 us; the launch traced here: 73.6 us
  Pallas kernels  71.8 us (97%)
  local copies, waits for them, and re-layouts  1.22 us (2%)
    pallas_call x1, Pallas kernels, on_device(): pl.pallas_call(functools.partial(gather_kernel, sizes, rows * nz * nx * 2...  54.9 us
    pallas_call x1, Pallas kernels, on_device(): pl.pallas_call(factor_kernel, out_shape=(jax.ShapeDtypeStruct((rows, RANK...  16.9 us

profile of v3, /device:TPU:1, one launch (start us, length us, event | category | flops | bytes accessed | tf_op | source)
XLA Modules:
  0.0 73.6 jit_solution(16503686597752165381)
XLA Ops:
  0.6 0.0 copy-start
  0.6 1.2 %copy-done = f32[2,16,64,128]{3,2,1,0:T(8,128)S(1)} copy-done((f32[2,16,64,128]{3,2,1,0:T(8,128)S(1)}, f32[2,16,64,128]{3,2,1,0:T(8,128)}, u32[]{:S(2)}) %copy-start) | copy-done | bytes 1048600
  1.9 54.9 %gather_gram.1 = (f32[4,2,16,16,128]{4,3,2,1,0:T(8,128)S(1)}, f32[2,16,40,128]{3,2,1,0:T(8,128)S(1)}) custom-call(f32[2,16,64,128]{3,2,1,0:T(8,128)S(1)} %copy-done), custom_call_target="tpu_custom_call" | custom-call | tf_op jit(solution)/shard_map/gather_gram/pallas_call | solution.py:418
  56.8 16.9 %factor_core.1 = (f32[512,128]{1,0:T(8,128)}, f32[512,128]{1,0:T(8,128)}) custom-call(f32[4,2,16,16,128]{4,3,2,1,0:T(8,128)S(1)} %get-tuple-element.6.fib, f32[1280,128]{1,0:T(8,128)S(1)} %bitcast.2), custom_call_target="tpu_custom_call" | custom-call | tf_op jit(solution)/shard_map/factor_core/pallas_call | solution.py:456
Async XLA Ops:
  0.6 1.2 %copy-start = (f32[2,16,64,128]{3,2,1,0:T(8,128)S(1)}, f32[2,16,64,128]{3,2,1,0:T(8,128)}, u32[]{:S(2)}) copy-start(f32[2,16,64,128]{3,2,1,0:T(8,128)} %field.1) | copy-start | bytes 3145732

commit v4 on v3

--- a/solution.py
+++ b/solution.py
@@ -65,6 +65,16 @@
 
     other = {"gy": x * 2 + (1 - c)}
 
+    def arrived(ref, sem):
+        pltpu.make_async_remote_copy(
+            src_ref=ref, dst_ref=ref, send_sem=sem, recv_sem=sem, device_id=other
+        ).wait_recv()
+
+    def left_here(ref, sem):
+        pltpu.make_async_remote_copy(
+            src_ref=ref, dst_ref=ref, send_sem=sem, recv_sem=sem, device_id=other
+        ).wait_send()
+
     barrier = pltpu.get_barrier_semaphore()
     near = [at_y(k) for k in range(1, ny)] + [other, at_x(1), at_x(-1), at_z(1), at_z(-1)]
     for device in near:
@@ -73,7 +83,6 @@
 
     deep = fib.shape[2] // 2
     chunks = [(s, pl.ds(h * deep, deep)) for s in range(steps) for h in range(2)]
-    sends = []
     order = sorted(range(1, ny), key=lambda k: -ring(ny, k))
     for n, (s, part) in enumerate(chunks):
         for k in order:
@@ -81,12 +90,11 @@
             copy = pltpu.make_async_remote_copy(
                 src_ref=field.at[s, part, pl.ds(to * cells, cells), :],
                 dst_ref=fib.at[y, s, part],
-                send_sem=a2a_send.at[n, k - 1],
-                recv_sem=a2a_recv.at[n, k - 1],
+                send_sem=a2a_send,
+                recv_sem=a2a_recv.at[n],
                 device_id={"gz": to},
             )
             copy.start()
-            sends.append(copy)
     owns = []
     for n, (s, part) in enumerate(chunks):
         copy = pltpu.make_async_copy(
@@ -103,10 +111,9 @@
             pl.semaphore_signal(known.at[i], inc=1, device_id=device)
         pl.semaphore_wait(known.at[i], len(devices))
 
-    for n, (s, _) in enumerate(chunks):
+    for n, (s, part) in enumerate(chunks):
         owns[n].wait()
-        for i in range(ny - 1):
-            sends[n * (ny - 1) + i].wait_recv()
+        arrived(fib.at[pl.ds(0, ny - 1), s, part], a2a_recv.at[n])
         x0 = (n % 2) * deep
         rows = jnp.concatenate([fib[b, s, x0 : x0 + deep].reshape(-1, LANES) for b in range(blocks)], axis=1)
         for i in range(0, blocks, 2):
@@ -130,38 +137,38 @@
     def rows_of(start, q):
         return pl.ds(pl.multiple_of(start + q * piece, 8), piece)
 
+    hops = [ring(nx, i) + ring(ny, j) for i, j in offsets] + [0]
+    groups = [[n for n in range(planes) if hops[n] == h] for h in range(max(hops), -1, -1)]
     keep = c * half_rows
     give = (1 - c) * half_rows
-    core_copies = []
     for n, (i, j) in enumerate(offsets + [(0, 0)]):
         q = plane_at(i, j)[0]
         copy = pltpu.make_async_remote_copy(
             src_ref=acc.at[rows_of(give, q)],
             dst_ref=core_in.at[rows_of(0, q)],
-            send_sem=core_send.at[n],
-            recv_sem=core_recv.at[n],
+            send_sem=core_send,
+            recv_sem=core_recv.at[hops[0] - hops[n]],
             device_id=other,
         )
         copy.start()
-        core_copies.append(copy)
-    plane_copies = []
     for n, (i, j) in enumerate(offsets):
         q, device = plane_at(i, j)
-        core_copies[n].wait_recv()
+        h = hops[0] - hops[n]
+        if n == groups[h][0]:
+            arrived(core_in.at[pl.ds(0, len(groups[h]) * piece)], core_recv.at[h])
         half[rows_of(0, q), :] = acc[rows_of(keep, q), :] + core_in[rows_of(0, q), :]
         copy = pltpu.make_async_remote_copy(
             src_ref=half.at[rows_of(0, q)],
             dst_ref=plane_in.at[n],
-            send_sem=plane_send.at[n],
-            recv_sem=plane_recv.at[n],
+            send_sem=plane_send,
+            recv_sem=plane_recv,
             device_id=device,
         )
         copy.start()
-        plane_copies.append(copy)
-    core_copies[-1].wait_recv()
+    arrived(core_in.at[pl.ds(0, piece)], core_recv.at[len(groups) - 1])
     total = acc[rows_of(keep, p), :] + core_in[rows_of(0, p), :]
-    for n in reversed(range(len(offsets))):
-        plane_copies[n].wait_recv()
+    arrived(plane_in, plane_recv)
+    for n in range(len(offsets)):
         total = total + plane_in[n]
     mine[...] = total
 
@@ -169,7 +176,6 @@
     keepers = [(t * spread % nz, (t * spread + nz // 2) % nz) for t in range(tiles)]
     assert len({v for pair in keepers for v in pair}) == 2 * tiles
     reach = sorted((k for k in range(1 - nz // 4, nz // 4 + 1) if k), key=lambda k: -ring(nz, k))
-    distances = sorted(range(1, nz), key=lambda k: ring(nz, k))
     keeps = [(z == a) | (z == b) for a, b in keepers]
     keeper = functools.reduce(lambda v, w: v | w, keeps)
     tile = sum(t * keeps[t].astype(jnp.int32) for t in range(tiles))
@@ -178,8 +184,8 @@
         return pltpu.make_async_remote_copy(
             src_ref=mine.at[pl.ds(t * 8, 8)],
             dst_ref=z_in.at[z],
-            send_sem=z_send.at[t, m],
-            recv_sem=z_recv.at[z],
+            send_sem=z_send,
+            recv_sem=z_recv,
             device_id={"gx": keepers[t][m]},
         )
 
@@ -187,7 +193,7 @@
         return pltpu.make_async_remote_copy(
             src_ref=z_sum.at[t],
             dst_ref=z_sum.at[t],
-            send_sem=zg_send.at[i],
+            send_sem=zg_send,
             recv_sem=zg_recv.at[t],
             device_id=at_z(reach[i]),
         )
@@ -202,15 +208,7 @@
     @pl.when(keeper)
     def _():
         z_in[z] = mine[pl.ds(pl.multiple_of(tile * 8, 8), 8), :]
-        for k in distances:
-            w = lax.rem(z + k, nz)
-            pltpu.make_async_remote_copy(
-                src_ref=z_in.at[w],
-                dst_ref=z_in.at[w],
-                send_sem=z_send.at[0, 0],
-                recv_sem=z_recv.at[w],
-                device_id={"gx": w},
-            ).wait_recv()
+        arrived(z_in.at[pl.ds(0, nz - 1)], z_recv)
         total = z_in[0]
         for w in range(1, nz):
             total = total + z_in[w]
@@ -226,50 +224,46 @@
 
     sums[c, p] = z_sum[...].reshape(piece, LANES)
 
-    def cg_copy(n, q):
+    def cg_copy(q):
         return pltpu.make_async_remote_copy(
             src_ref=sums.at[c, q],
             dst_ref=sums.at[c, q],
-            send_sem=cg_send.at[n],
-            recv_sem=cg_recv.at[n],
+            send_sem=cg_send,
+            recv_sem=cg_recv,
             device_id=other,
         )
 
-    pg_copies, cg_copies = [], []
     for n, (i, j) in enumerate(offsets):
-        copy = pltpu.make_async_remote_copy(
+        pltpu.make_async_remote_copy(
             src_ref=sums.at[c, p],
             dst_ref=sums.at[c, p],
-            send_sem=pg_send.at[n],
-            recv_sem=pg_recv.at[n],
+            send_sem=pg_send,
+            recv_sem=pg_recv.at[hops[0] - hops[n]],
             device_id=plane_at(i, j)[1],
-        )
-        copy.start()
-        pg_copies.append(copy)
-    cg_copies.append(cg_copy(len(offsets), p))
-    cg_copies[-1].start()
-    for n in reversed(range(len(offsets))):
-        i, j = offsets[n]
-        pg_copies[n].wait_recv()
-        cg_copies.append(cg_copy(n, plane_at(-i, -j)[0]))
-        cg_copies[-1].start()
-
-    for copy in sends + core_copies + plane_copies + pg_copies:
-        copy.wait_send()
-    for t in range(tiles):
-        for m in (0, 1):
-
-            @pl.when(z != keepers[t][m])
-            def _():
-                z_copy(t, m).wait_send()
+        ).start()
+    cg_copy(p).start()
+    for h in reversed(range(len(groups) - 1)):
+        arrived(sums.at[0, pl.ds(0, len(groups[h]))], pg_recv.at[h])
+        for n in groups[h]:
+            i, j = offsets[n]
+            cg_copy(plane_at(-i, -j)[0]).start()
+
+    left_here(fib.at[pl.ds(0, ny - 1)], a2a_send)
+    left_here(acc.at[pl.ds(0, half_rows)], core_send)
+    left_here(half.at[pl.ds(0, half_rows - piece)], plane_send)
+    left_here(sums.at[0, pl.ds(0, planes - 1)], pg_send)
 
     @pl.when(keeper)
     def _():
-        for i in range(len(reach)):
-            zg_copy(i, tile).wait_send()
-
-    for copy in cg_copies:
-        copy.wait()
+        left_here(z_in.at[pl.ds(0, 2 * tiles - 1)], z_send)
+        left_here(z_in.at[pl.ds(0, len(reach))], zg_send)
+
+    @pl.when(jnp.logical_not(keeper))
+    def _():
+        left_here(z_in.at[pl.ds(0, 2 * tiles)], z_send)
+
+    left_here(sums.at[0], cg_send)
+    arrived(sums.at[0], cg_recv)
 
 
 def reciprocal(d):
@@ -432,24 +426,24 @@
             pltpu.VMEM((nz, 8, LANES), f32),
             pltpu.VMEM((tiles, 8, LANES), f32),
             pltpu.SemaphoreType.REGULAR((3,)),
-            dma((2*steps,)),
-            dma((2*steps, ny - 1)),
-            dma((2*steps, ny - 1)),
-            dma((planes,)),
-            dma((planes,)),
-            dma((planes - 1,)),
-            dma((planes - 1,)),
-            dma((tiles, 2)),
-            dma((nz,)),
-            dma((nz // 2 - 1,)),
+            dma((2 * steps,)),
+            dma,
+            dma((2 * steps,)),
+            dma,
+            dma((nx // 2 + ny // 2 + 1,)),
+            dma,
+            dma,
+            dma,
+            dma,
+            dma,
             dma((tiles,)),
-            dma((planes - 1,)),
-            dma((planes - 1,)),
-            dma((planes,)),
-            dma((planes,)),
+            dma,
+            dma((nx // 2 + ny // 2,)),
+            dma,
+            dma,
         ],
         compiler_params=pltpu.CompilerParams(
-            collective_id=0, has_side_effects=True, vmem_limit_bytes=24 * 2**20
+            collective_id=0, has_side_effects=True, vmem_limit_bytes=52 * 2**20
         ),
         name="gather_gram",
     )(field)

time: 73.8 us -> 71.4 us (0.967)
  local copies, waits for them, and re-layouts: 1.22 us -> 0 us
  Pallas kernels: 71.8 us -> 70.6 us
    unnamed x2 -> x0, local copies, waits for them, and re-layouts: 1.22 us -> none
    pallas_call x1, Pallas kernels: 54.9 us -> 53.8 us  [on_device(): pl.pallas_call(functools.partial(gather_kernel, sizes, rows * nz * nx * 2...]
where the time goes in v4:
time: 71.4 us; the launch traced here: 71.3 us
  Pallas kernels  70.6 us (99%)
    pallas_call x1, Pallas kernels, on_device(): pl.pallas_call(functools.partial(gather_kernel, sizes, rows * nz * nx * 2...  53.8 us
    pallas_call x1, Pallas kernels, on_device(): pl.pallas_call(factor_kernel, out_shape=(jax.ShapeDtypeStruct((rows, RANK...  16.9 us

profile of v4, /device:TPU:1, one launch (start us, length us, event | category | flops | bytes accessed | tf_op | source)
XLA Modules:
  0.0 71.3 jit_solution(876113073865100500)
XLA Ops:
  0.6 53.8 %gather_gram.1 = (f32[4,2,16,16,128]{4,3,2,1,0:T(8,128)S(1)}, f32[2,16,40,128]{3,2,1,0:T(8,128)S(1)}) custom-call(f32[2,16,64,128]{3,2,1,0:T(8,128)} %field.1), custom_call_target="tpu_custom_call" | custom-call | tf_op jit(solution)/shard_map/gather_gram/pallas_call | solution.py:412
  54.4 16.9 %factor_core.1 = (f32[512,128]{1,0:T(8,128)}, f32[512,128]{1,0:T(8,128)}) custom-call(f32[4,2,16,16,128]{4,3,2,1,0:T(8,128)S(1)} %get-tuple-element.6.fib, f32[1280,128]{1,0:T(8,128)S(1)} %bitcast.2), custom_call_target="tpu_custom_call" | custom-call | tf_op jit(solution)/shard_map/factor_core/pallas_call | solution.py:450

commit v5 on v4

--- a/solution.py
+++ b/solution.py
@@ -75,15 +75,23 @@
             src_ref=ref, dst_ref=ref, send_sem=sem, recv_sem=sem, device_id=other
         ).wait_send()
 
+    deep = fib.shape[2] // 2
+    chunks = [(s, pl.ds(h * deep, deep)) for s in range(steps) for h in range(2)]
+    owns = []
+    for n, (s, part) in enumerate(chunks):
+        copy = pltpu.make_async_copy(
+            field.at[s, part, pl.ds(y * cells, cells), :], fib.at[y, s, part], own_sem.at[n]
+        )
+        copy.start()
+        owns.append(copy)
+
     barrier = pltpu.get_barrier_semaphore()
     near = [at_y(k) for k in range(1, ny)] + [other, at_x(1), at_x(-1), at_z(1), at_z(-1)]
     for device in near:
         pl.semaphore_signal(barrier, inc=1, device_id=device)
     pl.semaphore_wait(barrier, len(near))
 
-    deep = fib.shape[2] // 2
-    chunks = [(s, pl.ds(h * deep, deep)) for s in range(steps) for h in range(2)]
-    order = sorted(range(1, ny), key=lambda k: -ring(ny, k))
+    order = sorted(range(1, ny), key=lambda k: ring(ny, k))
     for n, (s, part) in enumerate(chunks):
         for k in order:
             to = lax.rem(y + k, ny)
@@ -95,14 +103,6 @@
                 device_id={"gz": to},
             )
             copy.start()
-    owns = []
-    for n, (s, part) in enumerate(chunks):
-        copy = pltpu.make_async_copy(
-            field.at[s, part, pl.ds(y * cells, cells), :], fib.at[y, s, part], own_sem.at[n]
-        )
-        copy.start()
-        owns.append(copy)
-
     rounds = [[at_x(1), at_x(-1), at_z(1), at_z(-1)], [at_z(2), at_z(-2)], [at_z(4), at_z(-4)]]
     if nx > 2:
         rounds[1].append(at_x(2))
@@ -116,8 +116,9 @@
         arrived(fib.at[pl.ds(0, ny - 1), s, part], a2a_recv.at[n])
         x0 = (n % 2) * deep
         rows = jnp.concatenate([fib[b, s, x0 : x0 + deep].reshape(-1, LANES) for b in range(blocks)], axis=1)
+        lhs, rhs = left(rows, 0), right(rows, 0)
         for i in range(0, blocks, 2):
-            term = full_dot(rows[:, i * LANES : (i + 2) * LANES], rows[:, i * LANES :], 0, 0)
+            term = short_dot(lhs[:, i * LANES : (i + 2) * LANES], rhs[:, i * LANES :], 0, 0)
             for a in (0, 1):
                 for b in range(i + a, blocks):
                     r = pairs.index((i + a, b)) * LANES

time: 71.4 us -> 70.8 us (level)
  no operation moved by 1% of the time
where the time goes in v5:
time: 70.8 us; the launch traced here: 70.7 us
  Pallas kernels  70 us (99%)
    pallas_call x1, Pallas kernels, on_device(): pl.pallas_call(functools.partial(gather_kernel, sizes, rows * nz * nx * 2...  53.2 us
    pallas_call x1, Pallas kernels, on_device(): pl.pallas_call(factor_kernel, out_shape=(jax.ShapeDtypeStruct((rows, RANK...  16.9 us

profile of v5, /device:TPU:1, one launch (start us, length us, event | category | flops | bytes accessed | tf_op | source)
XLA Modules:
  0.0 70.7 jit_solution(7187460557608296935)
XLA Ops:
  0.6 53.2 %gather_gram.1 = (f32[4,2,16,16,128]{4,3,2,1,0:T(8,128)S(1)}, f32[2,16,40,128]{3,2,1,0:T(8,128)S(1)}) custom-call(f32[2,16,64,128]{3,2,1,0:T(8,128)} %field.1), custom_call_target="tpu_custom_call" | custom-call | tf_op jit(solution)/shard_map/gather_gram/pallas_call | solution.py:413
  53.8 16.9 %factor_core.1 = (f32[512,128]{1,0:T(8,128)}, f32[512,128]{1,0:T(8,128)}) custom-call(f32[4,2,16,16,128]{4,3,2,1,0:T(8,128)S(1)} %get-tuple-element.6.fib, f32[1280,128]{1,0:T(8,128)S(1)} %bitcast.2), custom_call_target="tpu_custom_call" | custom-call | tf_op jit(solution)/shard_map/factor_core/pallas_call | solution.py:451

commit v6 on v5

--- a/solution.py
+++ b/solution.py
@@ -75,15 +75,15 @@
             src_ref=ref, dst_ref=ref, send_sem=sem, recv_sem=sem, device_id=other
         ).wait_send()
 
-    deep = fib.shape[2] // 2
-    chunks = [(s, pl.ds(h * deep, deep)) for s in range(steps) for h in range(2)]
-    owns = []
+    wide = fib.shape[2]
+    cuts = [(s, 0, wide) for s in range(steps - 1)]
+    cuts += [(steps - 1, 0, wide // 2), (steps - 1, wide // 2, wide // 4), (steps - 1, wide - wide // 4, wide // 4)]
+    chunks = [(s, pl.ds(x0, deep)) for s, x0, deep in cuts]
     for n, (s, part) in enumerate(chunks):
         copy = pltpu.make_async_copy(
-            field.at[s, part, pl.ds(y * cells, cells), :], fib.at[y, s, part], own_sem.at[n]
+            field.at[s, part, pl.ds(y * cells, cells), :], fib.at[y, s, part], own_sem
         )
         copy.start()
-        owns.append(copy)
 
     barrier = pltpu.get_barrier_semaphore()
     near = [at_y(k) for k in range(1, ny)] + [other, at_x(1), at_x(-1), at_z(1), at_z(-1)]
@@ -112,9 +112,10 @@
         pl.semaphore_wait(known.at[i], len(devices))
 
     for n, (s, part) in enumerate(chunks):
-        owns[n].wait()
+        if n == 0:
+            pltpu.make_async_copy(fib.at[0], fib.at[0], own_sem).wait()
         arrived(fib.at[pl.ds(0, ny - 1), s, part], a2a_recv.at[n])
-        x0 = (n % 2) * deep
+        x0, deep = cuts[n][1:]
         rows = jnp.concatenate([fib[b, s, x0 : x0 + deep].reshape(-1, LANES) for b in range(blocks)], axis=1)
         lhs, rhs = left(rows, 0), right(rows, 0)
         for i in range(0, blocks, 2):
@@ -427,9 +428,9 @@
             pltpu.VMEM((nz, 8, LANES), f32),
             pltpu.VMEM((tiles, 8, LANES), f32),
             pltpu.SemaphoreType.REGULAR((3,)),
-            dma((2 * steps,)),
-            dma,
-            dma((2 * steps,)),
+            dma,
+            dma,
+            dma((steps + 2,)),
             dma,
             dma((nx // 2 + ny // 2 + 1,)),
             dma,

time: 70.8 us -> 70.7 us (level)
  no operation moved by 1% of the time
where the time goes in v6:
time: 70.7 us; the launch traced here: 70.6 us
  Pallas kernels  70 us (99%)
    pallas_call x1, Pallas kernels, on_device(): pl.pallas_call(functools.partial(gather_kernel, sizes, rows * nz * nx * 2...  53.1 us
    pallas_call x1, Pallas kernels, on_device(): pl.pallas_call(factor_kernel, out_shape=(jax.ShapeDtypeStruct((rows, RANK...  16.9 us

profile of v6, /device:TPU:1, one launch (start us, length us, event | category | flops | bytes accessed | tf_op | source)
XLA Modules:
  0.0 70.6 jit_solution(16440374536897709232)
XLA Ops:
  0.6 53.1 %gather_gram.1 = (f32[4,2,16,16,128]{4,3,2,1,0:T(8,128)S(1)}, f32[2,16,40,128]{3,2,1,0:T(8,128)S(1)}) custom-call(f32[2,16,64,128]{3,2,1,0:T(8,128)} %field.1), custom_call_target="tpu_custom_call" | custom-call | tf_op jit(solution)/shard_map/gather_gram/pallas_call | solution.py:414
  53.7 16.9 %factor_core.1 = (f32[512,128]{1,0:T(8,128)}, f32[512,128]{1,0:T(8,128)}) custom-call(f32[4,2,16,16,128]{4,3,2,1,0:T(8,128)S(1)} %get-tuple-element.6.fib, f32[1280,128]{1,0:T(8,128)S(1)} %bitcast.2), custom_call_target="tpu_custom_call" | custom-call | tf_op jit(solution)/shard_map/factor_core/pallas_call | solution.py:452
